TPU v7x, 256 devices: a whole 4x4x8 slice. The times are simulated.
256 devices in a mesh: dp: 64 (over y, x_hi, z), tensor: 4 (over x_lo, core).
Axes of the slice: x: 4 (x_hi: 2, x_lo: 2; x = x_hi * 2 + x_lo), y: 4, z: 8, core: 2. Of those that a mesh axis runs over, the one named last changes fastest.
Arguments:
- tokens: bfloat16 [24576, 8192], P('dp', 'tensor'), may hold values from -6 to 6
- norm_gain: bfloat16 [8192], replicated, may hold values from 0.099609375 to 1.8984375
- q_weight: bfloat16 [8192, 2048], P('dp', 'tensor'), as said below
- key_value_weight: bfloat16 [8192, 2, 512], P('dp', None, 'tensor'), as said below
- output_weight: bfloat16 [2048, 8192], P('tensor', 'dp'), may hold values from -0.125 to 0.125
- lengths: int32 [64], P('dp'), may hold values from 1 to 384, as said below
Outputs:
- mixed: bfloat16 [24576, 8192], P('dp', 'tensor')
Inputs may be any that keep to these rules, and one draw needn't show every extreme that they name: The first lengths tokens of a sequence are valid; at least one sequence has all 384 valid. `key_value_weight`: independent entries of scale 8192 ** -0.5. `q_weight`: in one draw independent entries of order 8192 ** -0.5; in the other each query head is the key projection of its group times a per-head factor of 8 to 24, plus half an independent matrix of that scale.
All inputs are finite; a program needn't handle non-finite values.
Results may differ from a plain program's by a relative error of at most 0.013.
Values may be sent and summed in bfloat16 or wider, within the bound.
A program may use at most 128 MiB of HBM per device.

v0:
```python
import jax
import jax.numpy as jnp
from jax import lax
from jax.sharding import PartitionSpec as P


def apply_rotary(value_rows, token_positions):
    half = value_rows.shape[-1] // 2
    freqs = 500000.0 ** (-(jnp.arange(half, dtype=jnp.float32) * 2.0 / value_rows.shape[-1]))
    angles = token_positions[:, None] * freqs[None, :]
    cosine = jnp.cos(angles)[:, None, :]
    sine = jnp.sin(angles)[:, None, :]
    first = value_rows[..., :half]
    second = value_rows[..., half:]
    return jnp.concatenate(
        [first * cosine - second * sine, second * cosine + first * sine], axis=-1
    )


def per_device(tokens, norm_gain, q_weight, key_value_weight, output_weight, lengths):
    tok_rows = tokens.shape[0]
    seq_count = lengths.shape[0]
    seq_len = tok_rows // seq_count
    head_size = key_value_weight.shape[2]
    group_cols = q_weight.shape[1]
    group_heads = group_cols // head_size
    whole = lax.all_gather(tokens, "tensor", axis=1, tiled=True)
    wide = whole.astype(jnp.float32)
    msq = jnp.mean(wide * wide, axis=-1, keepdims=True)
    normed_input = (wide * lax.rsqrt(msq + 1e-05) * norm_gain.astype(jnp.float32)).astype(
        jnp.bfloat16
    )
    key_value_flat = key_value_weight.reshape(key_value_weight.shape[0], 2 * head_size)
    query_rows = jnp.dot(
        normed_input,
        lax.all_gather(q_weight, "dp", axis=0, tiled=True),
        preferred_element_type=jnp.float32,
    )
    key_value_pair = jnp.dot(
        normed_input,
        lax.all_gather(key_value_flat, "dp", axis=0, tiled=True),
        preferred_element_type=jnp.float32,
    )
    token_positions = jnp.tile(jnp.arange(seq_len, dtype=jnp.float32), seq_count)
    query_rows = query_rows.reshape(tok_rows, group_heads, head_size)
    key_value_pair = key_value_pair.reshape(tok_rows, 2, head_size)
    rotated_query = apply_rotary(query_rows, token_positions).astype(jnp.bfloat16)
    rk = apply_rotary(key_value_pair[:, 0:1, :], token_positions).astype(jnp.bfloat16)
    rv = key_value_pair[:, 1, :].astype(jnp.bfloat16)
    rotated_query = rotated_query.reshape(seq_count, seq_len, group_heads, head_size)
    rk = rk.reshape(seq_count, seq_len, head_size)
    rv = rv.reshape(seq_count, seq_len, head_size)
    scores = jnp.einsum(
        "sihd,sjd->shij", rotated_query, rk, preferred_element_type=jnp.float32
    ) / jnp.sqrt(jnp.float32(head_size))
    rows = jnp.arange(seq_len, dtype=jnp.int32)
    keep = (rows[None, None, :] <= rows[None, :, None]) & (
        rows[None, None, :] < lengths[:, None, None]
    )
    scores = jnp.where(keep[:, None], scores, jnp.float32(-1e30))
    top = jnp.max(scores, axis=-1, keepdims=True)
    expo = jnp.exp(scores - top)
    weights = (expo / jnp.sum(expo, axis=-1, keepdims=True)).astype(jnp.bfloat16)
    attended_output = jnp.einsum(
        "shij,sjd->sihd", weights, rv, preferred_element_type=jnp.float32
    ).astype(jnp.bfloat16)
    attended_output = attended_output.reshape(tok_rows, group_cols)
    terms = jnp.dot(
        attended_output,
        lax.all_gather(output_weight, "dp", axis=1, tiled=True),
        preferred_element_type=jnp.float32,
    )
    summed = lax.psum_scatter(
        terms.astype(jnp.bfloat16), "tensor", scatter_dimension=1, tiled=True
    ).astype(jnp.float32)
    return (summed + tokens.astype(jnp.float32)).astype(jnp.bfloat16)


def solution(mesh):
    return jax.shard_map(
        per_device,
        mesh=mesh,
        in_specs=(
            P("dp", "tensor"),
            P(),
            P("dp", "tensor"),
            P("dp", None, "tensor"),
            P("tensor", "dp"),
            P("dp"),
        ),
        out_specs=P("dp", "tensor"),
        check_vma=False,
    )
```

profile of v0, /device:TPU:1, one launch (start us, length us, event | category | flops | bytes accessed | tf_op | source)
XLA Modules:
  0.0 614.9 jit_solution(153239590309166875)
XLA Ops:
  6.5 0.0 all-gather.5.cloned.1.call-start
  6.5 0.7 all-gather.5.cloned.1.call-update
  7.3 0.0 all-gather.7.cloned.1.call-start
  7.3 1.5 copy.23
  8.8 0.0 all-gather.7.cloned.1.call-update
  8.8 0.0 all-gather.9.cloned.1.call-start
  8.9 0.7 all-gather.9.cloned.1.call-update
  9.5 0.0 all-gather.11.cloned.1.call-start
  9.6 0.5 all-gather.11.cloned.1.call-update
  10.1 0.0 reduce-scatter.2.cloned.1.call-start
  10.2 0.7 convert_element_type.48
  11.6 0.1 fusion.10
  11.7 0.7 fusion.16
  12.4 67.5 %all-gather.5.cloned.1.call-done = bf16[384,8192]{1,0:T(8,128)(2,1)} async-done(((bf16[384,2048]{1,0:T(8,128)(2,1)}), bf16[384,8192]{1,0:T(8,128)(2,1)}) %all-gather.5.cloned.1.call-update) | async-done | bytes 6291472 | tf_op jit(solution)/shard_map/all_gather | solution.py:27
  79.9 4.1 fusion
  84.0 124.6 %all-gather.7.cloned.1.call-done = bf16[8192,256]{1,0:T(8,128)(2,1)} async-done(((bf16[128,256]{1,0:T(8,128)(2,1)}), bf16[8192,256]{1,0:T(8,128)(2,1)}) %all-gather.7.cloned.1.call-update) | async-done | bytes 4194320 | tf_op jit(solution)/shard_map/all_gather | solution.py:41
  208.7 6.6 %fusion.6 = f32[384,256]{0,1:T(8,128)S(1)} fusion(bf16[8192,256]{1,0:T(8,128)(2,1)} %all-gather.7.cloned.1.call-done, bf16[384,8192]{1,0:T(8,128)(2,1)} %all-gather.5.cloned.1.call-done, f32[8192]{0:T(1024)S(1)} %convert_element_type.48, f32[384]{0:T(512)S(1)} %add_rsqrt_fusion), kind=kOutput, calls=%fused_computation.12 | convolution fusion | flops 1623195648 | bytes 10913280 | tf_op jit(solution)/shard_map/dot_general | solution.py:39
  215.3 0.1 copy.13
  215.4 0.1 copy.14
  215.6 0.8 fusion.19
  216.4 144.2 %all-gather.9.cloned.1.call-done = bf16[8192,512]{1,0:T(8,128)(2,1)} async-done(((bf16[128,512]{1,0:T(8,128)(2,1)}), bf16[8192,512]{1,0:T(8,128)(2,1)}) %all-gather.9.cloned.1.call-update) | async-done | bytes 8388624 | tf_op jit(solution)/shard_map/all_gather | solution.py:36
  360.6 7.9 %fusion.4 = f32[384,512]{1,0:T(8,128)S(1)} fusion(bf16[8192,512]{1,0:T(8,128)(2,1)} %all-gather.9.cloned.1.call-done, bf16[384,8192]{1,0:T(8,128)(2,1)} %all-gather.5.cloned.1.call-done, f32[8192]{0:T(1024)S(1)} %convert_element_type.48, f32[384]{0:T(512)S(1)} %add_rsqrt_fusion), kind=kOutput, calls=%fused_computation.11 | convolution fusion | flops 3233808384 | bytes 15500800 | tf_op jit(solution)/shard_map/dot_general | solution.py:34
  368.4 0.3 reshape.194
  368.7 0.5 fusion.28
  369.2 0.2 subtract_convert_fusion
  369.4 0.7 fusion.8
  370.1 0.5 fusion.3
  370.7 0.9 convolution_convert_fusion.1
  371.6 159.8 %all-gather.11.cloned.1.call-done = bf16[512,8192]{1,0:T(8,128)(2,1)} async-done(((bf16[512,128]{1,0:T(8,128)(2,1)}), bf16[512,8192]{1,0:T(8,128)(2,1)}) %all-gather.11.cloned.1.call-update) | async-done | bytes 8388624 | tf_op jit(solution)/shard_map/all_gather | solution.py:70
  531.3 9.5 %convolution_convert_fusion = bf16[384,8192]{1,0:T(8,128)(2,1)} fusion(bf16[384,512]{0,1:T(8,128)(2,1)S(1)} %bitcast.45, bf16[512,8192]{1,0:T(8,128)(2,1)} %all-gather.11.cloned.1.call-done), kind=kOutput, calls=%fused_computation.5 | convolution fusion | flops 3224371200 | bytes 15073280 | tf_op jit(solution)/shard_map/dot_general | solution.py:68
  540.9 0.0 copy-start
  540.9 0.0 reduce-scatter.2.cloned.1.call-update
  540.9 64.3 %reduce-scatter.2.cloned.1.call-done = bf16[384,2048]{1,0:T(8,128)(2,1)} async-done(((bf16[384,8192]{1,0:T(8,128)(2,1)}), bf16[384,2048]{1,0:T(8,128)(2,1)}) %reduce-scatter.2.cloned.1.call-update) | async-done | bytes 1572880 | tf_op jit(solution)/shard_map/reduce_scatter | solution.py:73
  605.2 0.0 copy-done
  605.2 3.2 add_convert_fusion
  (4 shorter events, 0.0 us)
Async XLA Ops:
  6.5 73.4 %all-gather.5.cloned.1.call-start = ((), (), s32[]{:S(2)}) async-start(), calls=%async_computation.1 | async-start | bytes 7864320 | tf_op jit(solution)/shard_map/all_gather | solution.py:27
  7.3 201.4 %all-gather.7.cloned.1.call-start = ((), (), s32[]{:S(2)}) async-start(), calls=%async_computation.2 | async-start | bytes 4259840 | tf_op jit(solution)/shard_map/all_gather | solution.py:41
  8.8 351.8 %all-gather.9.cloned.1.call-start = ((), (), s32[]{:S(2)}) async-start(), calls=%async_computation.3 | async-start | bytes 8519680 | tf_op jit(solution)/shard_map/all_gather | solution.py:36
  9.5 521.8 %all-gather.11.cloned.1.call-start = ((), (), s32[]{:S(2)}) async-start(), calls=%async_computation.4 | async-start | bytes 8519680 | tf_op jit(solution)/shard_map/all_gather | solution.py:70
  10.1 595.1 %reduce-scatter.2.cloned.1.call-start = ((), (), s32[]{:S(2)}) async-start(), calls=%async_computation.5 | async-start | bytes 7864320 | tf_op jit(solution)/shard_map/reduce_scatter | solution.py:73
  540.9 64.4 %copy-start = (bf16[384,2048]{1,0:T(8,128)(2,1)S(1)}, bf16[384,2048]{1,0:T(8,128)(2,1)}, u32[]{:S(2)}) copy-start(bf16[384,2048]{1,0:T(8,128)(2,1)} %param.6) | copy-start | bytes 4718596
Sparse Core Ops, SparseCore 0:
  9.2 70.7 all-gather.4
  83.4 125.1 all-gather.6
  212.3 148.2 all-gather.8
  363.8 167.4 all-gather.10
  541.0 64.1 reduce-scatter.1
where the time goes:
time: 615 us
  waiting for transfers between devices  562 us (91%)
  matrix products  25.6 us (4%)
  between operations  13.9 us (2%)
  other arithmetic  10.4 us (2%)
    all_gather x1, waiting for transfers between devices, per_device(): lax.all_gather(output_weight, 'dp', axis=1, tiled=True)  160 us
    all_gather x1, waiting for transfers between devices, per_device(): lax.all_gather(q_weight, 'dp', axis=0, tiled=True)  144 us
    all_gather x1, waiting for transfers between devices, per_device(): lax.all_gather(key_value_flat, 'dp', axis=0, tiled=True)  125 us
    all_gather x1, waiting for transfers between devices, per_device(): whole = lax.all_gather(tokens, 'tensor', axis=1, tiled=True)  67.5 us
    reduce_scatter x1, waiting for transfers between devices, per_device(): lax.psum_scatter(terms.astype(jnp.bfloat16), 'tensor', scatter_dimension=...  64.3 us
  transfers between devices with their start and end apart: 5, of which 5 were waited for; matrix products, arithmetic and copies ran while one was open for 4% of the time, Pallas kernels for 0%

commit v1 on v0

v1 whole, which is shorter than its diff:
```python
import functools

import jax
import jax.numpy as jnp
import numpy as np
from jax import lax
from jax.experimental import pallas as pl
from jax.experimental.pallas import tpu as pltpu
from jax.sharding import PartitionSpec as P

MESH = pl.DeviceIdType.MESH
SEQ = 384
HEAD = 128
HEADS = 4
FEATS = 2048
NY, NH, NZ = 4, 2, 8


def rotary_tables():
    half = HEAD // 2
    freqs = 500000.0 ** (-(np.arange(half, dtype=np.float64) * 2.0 / HEAD))
    angles = np.arange(SEQ, dtype=np.float64)[:, None] * freqs[None, :]
    cosine, sine = np.cos(angles), np.sin(angles)
    return (
        np.concatenate([cosine, cosine], axis=1).astype(np.float32),
        np.concatenate([-sine, sine], axis=1).astype(np.float32),
    )


def device(y, h, z, l, c):
    return (y * (NH * NZ) + h * NZ + z, l * 2 + c)


def kernel(
    tok, gain, w1_own, wo_own, len_own, cos, sin, out,
    xb, w1, wo, ab, aout, lenb, acc, ssq,
    t_ss, t_rs, t_fs, l_sem, e_ss, e_rs, n_ss, n_rs,
    z_ss, z_rs, y_ss, y_rs, c_ss, c_rs,
    ox_ss, ox_rs, oy_ss, oy_rs, oz_ss, oz_rs,
    a_ss, a_rs, b_ss, b_rs,
):
    dp = lax.axis_index("dp")
    tensor = lax.axis_index("tensor")
    y, h, z = dp // (NH * NZ), (dp // NZ) % NH, dp % NZ
    l, c = tensor // 2, tensor % 2
    x = 2 * h + l
    main = c == h
    yp, yn = (y + 1) % NY, (y + NY - 1) % NY

    def zat(k):
        return (z + k + NZ) % NZ

    def at_x(xx, cc):
        return device(y, xx // 2, z, xx % 2, cc)

    def remote(src, dst, ss, rs, dev):
        return pltpu.make_async_remote_copy(
            src_ref=src, dst_ref=dst, send_sem=ss, recv_sem=rs, device_id=dev, device_id_type=MESH
        )

    xnext, xprev = (x + 1) % 4, (x + 3) % 4
    sibling = device(y, h, z, l, 1 - c)
    z_dev = (device(y, h, zat(1), l, c), device(y, h, zat(-1), l, c))
    y_dev = (device(yp, h, z, l, c), device(yn, h, z, l, c))

    barrier = pltpu.get_barrier_semaphore()
    partners = [sibling, *z_dev, *y_dev]
    for k in (1, 2, 3):
        for cc in (0, 1):
            partners.append(at_x((x + k) % 4, cc))
    for p in partners:
        pl.semaphore_signal(barrier, inc=1, device_id=p, device_id_type=MESH)
    pl.semaphore_wait(barrier, len(partners))

    me1 = y * 16 + c * 8 + z
    partner = device(y, 1 - h, z, l, 1 - c)
    exchange = remote(w1_own, w1.at[y * 16 + (1 - c) * 8 + z], e_ss.at[0], e_rs.at[0], partner)
    exchange_in = remote(w1_own, w1.at[me1], e_ss.at[0], e_rs.at[0], partner)
    len_out = remote(len_own, lenb, n_ss.at[0], n_rs.at[0], partner)
    own1 = pltpu.make_async_copy(w1_own, w1.at[me1], l_sem.at[0])
    own_len = pltpu.make_async_copy(len_own, lenb, l_sem.at[1])

    @pl.when(main)
    def _():
        own1.start()
        own_len.start()

    @pl.when(jnp.logical_not(main))
    def _():
        exchange.start()
        len_out.start()

    own_t = 2 * l + c
    source = own_t == y
    ox_dev = [device(y, hd, z, y // 2, y % 2) for hd in (0, 1)]
    ox_self = [jnp.logical_and(source, h == hd) for hd in (0, 1)]
    ox = [remote(wo_own, wo.at[z, h, own_t], ox_ss.at[hd], ox_rs.at[h, own_t], ox_dev[hd]) for hd in (0, 1)]
    own_o = pltpu.make_async_copy(wo_own, wo.at[z, h, own_t], l_sem.at[2])
    for hd in (0, 1):
        @pl.when(jnp.logical_not(ox_self[hd]))
        def _():
            ox[hd].start()

    @pl.when(source)
    def _():
        own_o.start()

    half = SEQ // 2

    def rows(k):
        return pl.ds(k * half, half)

    r = (x + 4 - 2 * c) % 4
    up = jnp.logical_or(r == 1, r == 2)
    fwd_half = jnp.where(r >= 2, 1, 0)

    def tok_copy(dst_x, k, i):
        return remote(tok.at[rows(k)], xb.at[own_t, rows(k)], t_ss.at[i, k], t_rs.at[own_t, k], at_x(dst_x, h))

    pair_x = jnp.where(l == 0, xnext, xprev)
    outer_x = jnp.where(l == 0, xprev, xnext)
    own_tok = pltpu.make_async_copy(tok, xb.at[own_t], l_sem.at[3])
    tok_copy(pair_x, 0, 0).start()
    tok_copy(outer_x, 1, 1).start()
    tok_copy(pair_x, 1, 0).start()
    tok_copy(outer_x, 0, 1).start()

    @pl.when(main)
    def _():
        own_tok.start()

    @pl.when(jnp.logical_not(main))
    def _():
        tok_copy(x, 0, 2).start()
        tok_copy(x, 1, 2).start()

    def got_tok(f, k):
        return remote(tok.at[rows(k)], xb.at[f, rows(k)], t_ss.at[0, k], t_rs.at[f, k], sibling)

    near_pair = jnp.where(jnp.logical_or(r == 0, r == 2), 1, 0)
    fwd_x = jnp.where(up, xnext, xprev)

    def tok_forward(j):
        f = 2 * near_pair + j
        piece = xb.at[f, pl.ds(pl.multiple_of(fwd_half * half, half), half)]
        return remote(piece, piece, t_fs.at[j], t_rs.at[f, fwd_half], at_x(fwd_x, c))

    def z_piece(origin, s, d):
        b = w1.at[y * 16 + c * 8 + origin]
        if s == 4:
            b = b.at[pl.ds(64 * d, 64)]
        return b

    def w1_z(s, d):
        origin = zat(-(s - 1)) if d == 0 else zat(s - 1)
        b = z_piece(origin, s, d)
        return remote(b, b, z_ss.at[d, s - 1], z_rs.at[d, s - 1], z_dev[d])

    def w1_z_in(s, d):
        origin = zat(-s) if d == 0 else zat(s)
        b = z_piece(origin, s, d)
        return remote(b, b, z_ss.at[d, s - 1], z_rs.at[d, s - 1], z_dev[d])

    @pl.when(main)
    def _():
        own1.wait()

    @pl.when(jnp.logical_not(main))
    def _():
        exchange_in.wait_recv()

    for d in (0, 1):
        w1_z(1, d).start()

    rel = (y + NY - own_t) % NY

    def oy(d, k):
        b = wo.at[z, k]
        return remote(b, b, oy_ss.at[d, k], oy_rs.at[k], y_dev[d])

    @pl.when(rel == 0)
    def _():
        own_o.wait()
        for hs in (0, 1):
            for t in range(4):
                @pl.when(jnp.logical_not(jnp.logical_and(hs == h, t == own_t)))
                def _():
                    remote(wo_own, wo.at[z, hs, t], ox_ss.at[0], ox_rs.at[hs, t], sibling).wait_recv()
        oy(0, 0).start()
        oy(1, 1).start()
        oy(0, 1).start()
        oy(1, 0).start()

    for s in (2, 3, 4):
        for d in (0, 1):
            w1_z_in(s - 1, d).wait_recv()
            w1_z(s, d).start()

    @pl.when(rel == 1)
    def _():
        oy(0, 0).wait_recv()
        oy(0, 0).start()

    @pl.when(rel == 3)
    def _():
        oy(0, 1).wait_recv()
        oy(1, 1).start()

    for j in (0, 1):
        got_tok(2 * near_pair + j, fwd_half).wait_recv()
        tok_forward(j).start()

    for d in (0, 1):
        w1_z_in(4, d).wait_recv()

    def plane(yy, core, k=None):
        if k is None:
            return w1.at[pl.ds(yy * 16 + core * 8, 8)]
        return w1.at[pl.ds(yy * 16 + core * 8 + 4 * k, 4)]

    def share(b, i):
        return remote(b, b, c_ss.at[i], c_rs.at[i], sibling)

    def w1_y(d, k):
        b = plane(y, c, k)
        return remote(b, b, y_ss.at[d, k], y_rs.at[d, k], y_dev[d])

    def w1_y_fwd(d):
        b = plane(yn if d == 0 else yp, c, d)
        return remote(b, b, y_ss.at[d, 2], y_rs.at[d, 2], y_dev[d])

    def w1_y_in(d, k):
        yy = yn if d == 0 else yp
        b = plane(yy, c, k)
        return remote(b, b, y_ss.at[d, k], y_rs.at[d, k], y_dev[d])

    yf = (y + 2) % NY

    def w1_y_far(d):
        b = plane(yf, c, d)
        return remote(b, b, y_ss.at[d, 2], y_rs.at[d, 2], y_dev[d])

    w1_y(0, 0).start()
    w1_y(1, 1).start()
    w1_y(0, 1).start()
    w1_y(1, 0).start()
    share(plane(y, c), 0).start()

    def oz_out(s, d, k):
        origin = zat(-(s - 1)) if d == 0 else zat(s - 1)
        b = wo.at[origin, k]
        return remote(b, b, oz_ss.at[d, s - 1, k], oz_rs.at[d, s - 1, k], z_dev[d])

    def oz_in(s, d, k):
        origin = zat(-s) if d == 0 else zat(s)
        b = wo.at[origin, k]
        return remote(b, b, oz_ss.at[d, s - 1, k], oz_rs.at[d, s - 1, k], z_dev[d])

    @pl.when(rel == 1)
    def _():
        oy(0, 1).wait_recv()

    @pl.when(rel == 3)
    def _():
        oy(0, 0).wait_recv()

    @pl.when(rel == 2)
    def _():
        oy(0, 0).wait_recv()
        oy(0, 1).wait_recv()

    def oz_step(s):
        for k in (0, 1):
            for d in (0, 1):
                if s > 1:
                    oz_in(s - 1, d, k).wait_recv()
                if s < 4 or d == k:
                    oz_out(s, d, k).start()

    oz_step(1)

    acc[...] = jnp.zeros_like(acc)
    ssq[...] = jnp.zeros_like(ssq)

    def project(f):
        def body(i, _):
            cols = pl.ds(pl.multiple_of(i * 512, 512), 512)
            xf = xb[f, :, cols].astype(jnp.float32)
            sq = xf * xf
            ssq[...] += sq[:, :128] + sq[:, 128:256] + sq[:, 256:384] + sq[:, 384:]
            xg = (xf * gain[f, :, cols]).astype(jnp.bfloat16)
            w = w1[pl.ds(f * 16 + i * 4, 4)].reshape(512, 768)
            acc[...] += jnp.dot(xg, w, preferred_element_type=jnp.float32)
            return 0

        lax.fori_loop(0, 4, body, 0)

    w1_y_in(0, 0).wait_recv()
    w1_y_fwd(0).start()
    w1_y_in(1, 1).wait_recv()
    w1_y_fwd(1).start()
    share(plane(yn, c, 0), 1).start()
    share(plane(yp, c, 1), 2).start()

    oz_step(2)

    @pl.when(main)
    def _():
        own_tok.wait()

    for f in range(4):
        for k in (0, 1):
            here = jnp.logical_and(main, f == own_t)
            handed = jnp.logical_and(f // 2 == near_pair, k == fwd_half)

            @pl.when(jnp.logical_not(jnp.logical_or(here, handed)))
            def _():
                got_tok(f, k).wait_recv()

    share(plane(y, 1 - c), 0).wait_recv()
    project(y)

    w1_y_in(0, 1).wait_recv()
    share(plane(yn, c, 1), 3).start()
    w1_y_in(1, 0).wait_recv()
    share(plane(yp, c, 0), 4).start()
    share(plane(yn, 1 - c, 0), 1).wait_recv()
    share(plane(yn, 1 - c, 1), 3).wait_recv()
    project(yn)
    share(plane(yp, 1 - c, 1), 2).wait_recv()
    share(plane(yp, 1 - c, 0), 4).wait_recv()
    project(yp)

    oz_step(3)

    for d in (0, 1):
        w1_y_far(d).wait_recv()
        share(plane(yf, c, d), 5 + d).start()
    for d in (0, 1):
        share(plane(yf, 1 - c, d), 5 + d).wait_recv()
    project(yf)

    @pl.when(main)
    def _():
        own_len.wait()

    @pl.when(jnp.logical_not(main))
    def _():
        remote(len_own, lenb, n_ss.at[0], n_rs.at[0], partner).wait_recv()

    rs = lax.rsqrt(jnp.sum(ssq[...], axis=1, keepdims=True) * (1.0 / 8192.0) + 1e-05)

    def rotate(v):
        return (v * cos[...] + pltpu.roll(v, 64, 1) * sin[...]).astype(jnp.bfloat16)

    rk = rotate(acc[:, 512:640] * rs)
    rv = (acc[:, 640:768] * rs).astype(jnp.bfloat16)
    i_pos = lax.broadcasted_iota(jnp.int32, (SEQ, SEQ), 0)
    j_pos = lax.broadcasted_iota(jnp.int32, (SEQ, SEQ), 1)
    keep = jnp.logical_and(j_pos <= i_pos, j_pos < lenb[0:1, 0:1])
    scale = 1.0 / float(np.sqrt(128.0))
    t_here = 2 * l + h

    def a_self(ld):
        return jnp.logical_and(main, l == ld)

    def a_out(ld, hd):
        return remote(aout.at[hd], ab.at[t_here, hd], a_ss.at[ld, hd], a_rs.at[t_here, hd], device(y, c, z, ld, c))

    def a_in(t, hd):
        return remote(aout.at[hd], ab.at[t, hd], a_ss.at[0, hd], a_rs.at[t, hd], sibling)

    def b_copy(t, hd):
        return remote(ab.at[t, hd], ab.at[t, hd], b_ss.at[t, hd], b_rs.at[t, hd], sibling)

    for hd in range(HEADS):
        rq = rotate(acc[:, hd * HEAD : (hd + 1) * HEAD] * rs)
        s = lax.dot_general(rq, rk, (((1,), (1,)), ((), ())), preferred_element_type=jnp.float32) * scale
        s = jnp.where(keep, s, jnp.float32(-1e30))
        e = jnp.exp(s - jnp.max(s, axis=1, keepdims=True))
        total = jnp.sum(e, axis=1, keepdims=True)
        o = jnp.dot(e.astype(jnp.bfloat16), rv, preferred_element_type=jnp.float32) / total
        o = o.astype(jnp.bfloat16)
        aout[hd] = o
        for ld in (0, 1):
            @pl.when(jnp.logical_not(a_self(ld)))
            def _():
                a_out(ld, hd).start()

        @pl.when(main)
        def _():
            ab[t_here, hd] = o
            b_copy(t_here, hd).start()

    oz_step(4)

    for t in range(4):
        for hd in range(HEADS):
            @pl.when(jnp.logical_and(main, t != t_here))
            def _():
                a_in(t, hd).wait_recv()
                b_copy(t, hd).start()

            @pl.when(jnp.logical_not(main))
            def _():
                b_copy(t, hd).wait_recv()

    def project_out(zz):
        total = jnp.zeros((SEQ, 256), jnp.float32)
        for t in range(4):
            a = jnp.concatenate([ab[t, hd] for hd in range(HEADS)], axis=1)
            w = jnp.concatenate([wo[zz, 0, t], wo[zz, 1, t]], axis=1)
            total += jnp.dot(a, w, preferred_element_type=jnp.float32)
        for hh in (0, 1):
            cols = pl.ds(pl.multiple_of(hh * 1024 + zz * 128, 128), 128)
            out[:, cols] = (total[:, hh * 128 : (hh + 1) * 128] + tok[:, cols].astype(jnp.float32)).astype(jnp.bfloat16)

    def out_body(i, _):
        project_out((z + i + NZ - 3) % NZ)
        return 0

    lax.fori_loop(0, 7, out_body, 0)
    oz_in(4, 0, 0).wait_recv()
    oz_in(4, 1, 1).wait_recv()
    project_out(zat(4))

    @pl.when(jnp.logical_not(main))
    def _():
        exchange.wait_send()
        len_out.wait_send()
        tok_copy(x, 0, 2).wait_send()
        tok_copy(x, 1, 2).wait_send()

    for hd in (0, 1):
        @pl.when(jnp.logical_not(ox_self[hd]))
        def _():
            ox[hd].wait_send()
    for k in (0, 1):
        tok_copy(pair_x, k, 0).wait_send()
        tok_copy(outer_x, k, 1).wait_send()
        tok_forward(k).wait_send()
        w1_y_fwd(k).wait_send()
        for d in (0, 1):
            w1_y(d, k).wait_send()
            for s in (1, 2, 3):
                oz_out(s, d, k).wait_send()
        oz_out(4, k, k).wait_send()
    for s in (1, 2, 3, 4):
        for d in (0, 1):
            w1_z(s, d).wait_send()
    share(plane(y, c), 0).wait_send()
    for i in range(1, 7):
        share(plane(y, c, 0), i).wait_send()

    @pl.when(rel == 0)
    def _():
        for d in (0, 1):
            for k in (0, 1):
                oy(d, k).wait_send()

    @pl.when(rel == 1)
    def _():
        oy(0, 0).wait_send()

    @pl.when(rel == 3)
    def _():
        oy(1, 1).wait_send()

    for hd in range(HEADS):
        for ld in (0, 1):
            @pl.when(jnp.logical_not(a_self(ld)))
            def _():
                a_out(ld, hd).wait_send()

        @pl.when(main)
        def _():
            for t in range(4):
                b_copy(t, hd).wait_send()


def per_device(tokens, norm_gain, q_weight, key_value_weight, output_weight, lengths):
    w1_own = jnp.concatenate([q_weight, key_value_weight.reshape(128, 256)], axis=1)
    gain = norm_gain.astype(jnp.float32).reshape(4, 1, FEATS)
    len_own = jnp.broadcast_to(lengths.reshape(1, 1), (8, 128))
    cosine, sine = rotary_tables()
    dma = pltpu.SemaphoreType.DMA
    vmem = pl.BlockSpec(memory_space=pltpu.VMEM)
    bf16 = jnp.bfloat16
    return pl.pallas_call(
        kernel,
        out_shape=jax.ShapeDtypeStruct((SEQ, FEATS), bf16),
        in_specs=[vmem] * 7,
        out_specs=vmem,
        scratch_shapes=[
            pltpu.VMEM((4, SEQ, FEATS), bf16),
            pltpu.VMEM((64, 128, 768), bf16),
            pltpu.VMEM((NZ, 2, 4, 512, 128), bf16),
            pltpu.VMEM((4, HEADS, SEQ, HEAD), bf16),
            pltpu.VMEM((HEADS, SEQ, HEAD), bf16),
            pltpu.VMEM((8, 128), jnp.int32),
            pltpu.VMEM((SEQ, 768), jnp.float32),
            pltpu.VMEM((SEQ, 128), jnp.float32),
            dma((3, 2)), dma((4, 2)), dma((2,)), dma((4,)), dma((1,)), dma((1,)), dma((1,)), dma((1,)),
            dma((2, 4)), dma((2, 4)), dma((2, 3)), dma((2, 3)), dma((7,)), dma((7,)),
            dma((2,)), dma((2, 4)), dma((2, 2)), dma((2,)), dma((2, 4, 2)), dma((2, 4, 2)),
            dma((2, HEADS)), dma((4, HEADS)), dma((4, HEADS)), dma((4, HEADS)),
        ],
        compiler_params=pltpu.CompilerParams(
            collective_id=0, has_side_effects=True, vmem_limit_bytes=56 * 2**20
        ),
        cost_estimate=pl.CostEstimate(flops=8 * 10**9, bytes_accessed=4 * 2**20, transcendentals=600000),
    )(tokens, gain, w1_own, output_weight, len_own, jnp.asarray(cosine), jnp.asarray(sine))


def solution(mesh):
    return jax.shard_map(
        per_device,
        mesh=mesh,
        in_specs=(
            P("dp", "tensor"),
            P(),
            P("dp", "tensor"),
            P("dp", None, "tensor"),
            P("tensor", "dp"),
            P("dp"),
        ),
        out_specs=P("dp", "tensor"),
        check_vma=False,
    )
```

time: 615 us -> 131 us (0.21)
  waiting for transfers between devices: 562 us -> 0 us
  Pallas kernels: 0 us -> 122 us
  matrix products: 25.6 us -> 0 us
  between operations: 13.9 us -> 0.66 us
  other arithmetic: 10.4 us -> 2.91 us
    all_gather x4 -> x0, waiting for transfers between devices: 496 us -> none  [the longest x1 160 us: per_device(): lax.all_gather(output_weight, 'dp', axis=1, tiled=True)]
    pallas_call x0 -> x1, Pallas kernels: none -> 122 us  [per_device(): pl.pallas_call(kernel, out_shape=jax.ShapeDtypeStruct((SEQ, FEATS), bf16)...]
    reduce_scatter x1 -> x0, waiting for transfers between devices: 64.3 us -> none  [per_device(): lax.psum_scatter(terms.astype(jnp.bfloat16), 'tensor', scatter_dimension=...]
    dot_general x5 -> x0, matrix products: 25.6 us -> none  [the longest x1 9.55 us: per_device(): jnp.dot(attended_output, lax.all_gather(output_weight, 'dp', axis=1, tile...]
  transfers between devices with their start and end apart: 5 -> 0, of which waited for: 5 -> 0; matrix products, arithmetic and copies ran while one was open for 4% -> 0% of each run, Pallas kernels for 0% -> 0%
where the time goes in v1:
time: 131 us; the launch traced here: 130 us
  Pallas kernels  122 us (93%)
  local copies, waits for them, and re-layouts  4.17 us (3%)
  other arithmetic  2.91 us (2%)
    pallas_call x1, Pallas kernels, per_device(): pl.pallas_call(kernel, out_shape=jax.ShapeDtypeStruct((SEQ, FEATS), bf16)...  122 us
    unnamed x2, local copies, waits for them, and re-layouts  3.58 us

profile of v1, /device:TPU:1, one launch (start us, length us, event | category | flops | bytes accessed | tf_op | source)
XLA Modules:
  0.0 129.8 jit_solution(4612921438680260416)
XLA Ops:
  0.7 0.6 broadcast_in_dim.8.len_own
  1.2 1.3 %reshape.13 = f32[8192]{0:T(1024)} convert(bf16[8192]{0:T(1024)(128)(2,1)} %param.9) | non-fusion elementwise | flops 8192 | bytes 49152 | tf_op jit(solution)/shard_map/reshape | solution.py:483
  2.6 0.8 copy.11
  3.4 1.6 %pad_maximum_fusion.w1_own = bf16[128,768]{1,0:T(8,128)(2,1)} fusion(bf16[128,256]{1,0:T(8,128)(2,1)S(1)} %bitcast.7, bf16[128,512]{1,0:T(8,128)(2,1)} %param.10), kind=kLoop, calls=%fused_computation | loop fusion | flops 393216 | bytes 393216 | tf_op jit(solution)/shard_map/concatenate | solution.py:482
  5.0 122.0 %shard_map.82 = bf16[384,2048]{1,0:T(8,128)(2,1)} custom-call(bf16[384,2048]{1,0:T(8,128)(2,1)} %tok.1, f32[4,1,2048]{2,1,0:T(1,128)} %bitcast.9, bf16[128,768]{1,0:T(8,128)(2,1)} %pad_maximum_fusion.w1_own, bf16[512,128]{1,0:T(8,128)(2,1)} %wo_own.1, s32[8,128]{1,0:T(8,128)} %broadcast_in_dim.8.len_own, f32[384,128]{1,0:T(8,128)} %constant.4.clone.cos, ...), custom_call_target="tpu_custom_call" | custom-call | flops 8000000000 | bytes 4194304 | tf_op jit(solution)/shard_map/pallas_call | solution.py:489
  127.0 2.7 %copy.14 = bf16[384,2048]{1,0:T(8,128)(2,1)} copy(bf16[384,2048]{1,0:T(8,128)(2,1)} %shard_map.82) | data formatting | bytes 3145728

commit v2 on v1

v2 whole, which is shorter than its diff:
```python
import functools

import jax
import jax.numpy as jnp
import numpy as np
from jax import lax
from jax.experimental import pallas as pl
from jax.experimental.pallas import tpu as pltpu
from jax.sharding import PartitionSpec as P

MESH = pl.DeviceIdType.MESH
SEQ = 384
HEAD = 128
HEADS = 4
FEATS = 2048
NY, NH, NZ = 4, 2, 8


def rotary_tables():
    half = HEAD // 2
    freqs = 500000.0 ** (-(np.arange(half, dtype=np.float64) * 2.0 / HEAD))
    angles = np.arange(SEQ, dtype=np.float64)[:, None] * freqs[None, :]
    cosine, sine = np.cos(angles), np.sin(angles)
    return (
        np.concatenate([cosine, cosine], axis=1).astype(np.float32),
        np.concatenate([-sine, sine], axis=1).astype(np.float32),
    )


def device(y, h, z, l, c):
    return (y * (NH * NZ) + h * NZ + z, l * 2 + c)


def kernel(
    tok, gain_in, q_own, kv_own, wo_own, length, cos, sin, out,
    tok_own, gain, w1_own, len_own, xb, w1, wo, ab, aout, lenb, acc, ssq, mixed,
    t_ss, t_rs, t_fs, l_sem, e_ss, e_rs, n_ss, n_rs,
    z_ss, z_rs, y_ss, y_rs, f_ss, f_rs, c_ss, c_rs,
    ox_ss, ox_rs, oy_ss, oy_rs, oz_ss, oz_rs,
    q_ss, q_rs, gz_ss, gz_rs, gy_ss, gy_rs, x2_ss, x2_rs,
    a_ss, a_rs, b_ss, b_rs,
):
    dp = lax.axis_index("dp")
    tensor = lax.axis_index("tensor")
    y, h, z = dp // (NH * NZ), (dp // NZ) % NH, dp % NZ
    l, c = tensor // 2, tensor % 2
    x = 2 * h + l
    main = c == h
    yp, yn = (y + 1) % NY, (y + NY - 1) % NY

    def zat(k):
        return (z + k + NZ) % NZ

    def at_x(xx, cc):
        return device(y, xx // 2, z, xx % 2, cc)

    def remote(src, dst, ss, rs, dev):
        return pltpu.make_async_remote_copy(
            src_ref=src, dst_ref=dst, send_sem=ss, recv_sem=rs, device_id=dev, device_id_type=MESH
        )

    xnext, xprev = (x + 1) % 4, (x + 3) % 4
    sibling = device(y, h, z, l, 1 - c)
    z_dev = (device(y, h, zat(1), l, c), device(y, h, zat(-1), l, c))
    y_dev = (device(yp, h, z, l, c), device(yn, h, z, l, c))

    barrier = pltpu.get_barrier_semaphore()
    partners = [sibling, *z_dev, *y_dev, device((y + 2) % NY, h, z, l, c)]
    for k in (1, 2, 3):
        for cc in (0, 1):
            partners.append(at_x((x + k) % 4, cc))
    for p in partners:
        pl.semaphore_signal(barrier, inc=1, device_id=p, device_id_type=MESH)
    pl.semaphore_wait(barrier, len(partners))

    w1_own[:, :512] = q_own[...]
    w1_own[:, 512:640] = kv_own[:, 0, :]
    w1_own[:, 640:] = kv_own[:, 1, :]
    len_own[...] = jnp.full((8, 128), length[0], jnp.int32)
    me1 = y * 16 + c * 8 + z
    partner = device(y, 1 - h, z, l, 1 - c)
    exchange = remote(w1_own, w1.at[y * 16 + (1 - c) * 8 + z], e_ss.at[0], e_rs.at[0], partner)
    exchange_in = remote(w1_own, w1.at[me1], e_ss.at[0], e_rs.at[0], partner)
    len_out = remote(len_own, lenb, n_ss.at[0], n_rs.at[0], partner)
    own1 = pltpu.make_async_copy(w1_own, w1.at[me1], l_sem.at[0])
    own_len = pltpu.make_async_copy(len_own, lenb, l_sem.at[1])

    @pl.when(main)
    def _():
        own1.start()
        own_len.start()

    @pl.when(jnp.logical_not(main))
    def _():
        exchange.start()
        len_out.start()

    own_t = 2 * l + c
    rel = (y + NY - own_t) % NY
    source = rel == 0
    ox_dev = [device(y, hd, z, y // 2, y % 2) for hd in (0, 1)]
    own_u = wo.at[jnp.where(own_t == 3, NZ, z), 2 * own_t + h]
    ox = [remote(wo_own, own_u, ox_ss.at[hd], ox_rs.at[2 * own_t + h], ox_dev[hd]) for hd in (0, 1)]
    own_o = pltpu.make_async_copy(wo_own, own_u, l_sem.at[2])
    for hd in (0, 1):
        @pl.when(jnp.logical_not(jnp.logical_and(source, h == hd)))
        def _():
            ox[hd].start()

    @pl.when(source)
    def _():
        own_o.start()

    half = SEQ // 2

    def rows(k):
        return pl.ds(k * half, half)

    r = (x + 4 - 2 * c) % 4
    up = jnp.logical_or(r == 1, r == 2)
    fwd_half = jnp.where(r >= 2, 1, 0)

    def tok_copy(dst_x, k, i):
        return remote(tok.at[rows(k)], xb.at[own_t, rows(k)], t_ss.at[i, k], t_rs.at[own_t, k], at_x(dst_x, h))

    pair_x = jnp.where(l == 0, xnext, xprev)
    outer_x = jnp.where(l == 0, xprev, xnext)
    own_tok = pltpu.make_async_copy(tok, xb.at[own_t], l_sem.at[3])
    keep_tok = pltpu.make_async_copy(tok, tok_own, l_sem.at[4])
    tok_copy(pair_x, 0, 0).start()
    tok_copy(outer_x, 1, 1).start()
    tok_copy(pair_x, 1, 0).start()
    tok_copy(outer_x, 0, 1).start()

    @pl.when(main)
    def _():
        own_tok.start()

    @pl.when(jnp.logical_not(main))
    def _():
        tok_copy(x, 0, 2).start()
        tok_copy(x, 1, 2).start()

    def got_tok(f, k):
        return remote(tok.at[rows(k)], xb.at[f, rows(k)], t_ss.at[0, k], t_rs.at[f, k], sibling)

    near_pair = jnp.where(jnp.logical_or(r == 0, r == 2), 1, 0)
    fwd_x = jnp.where(up, xnext, xprev)

    def tok_forward(j):
        f = 2 * near_pair + j
        piece = xb.at[f, pl.ds(pl.multiple_of(fwd_half * half, half), half)]
        return remote(piece, piece, t_fs.at[j], t_rs.at[f, fwd_half], at_x(fwd_x, c))

    def blk(yy, origin):
        return w1.at[yy * 16 + c * 8 + origin]

    def halves(b, d):
        return b.at[pl.ds(64 * d, 64)]

    def ring(cut, piece, ss, rs):
        def at(origin, s, d):
            b = piece(origin)
            return cut(b, d) if s == 4 else b

        def send(s, d):
            b = at(zat(1 - s) if d == 0 else zat(s - 1), s, d)
            return remote(b, b, ss.at[d, s - 1], rs.at[d, s - 1], z_dev[d])

        def take(s, d):
            b = at(zat(-s) if d == 0 else zat(s), s, d)
            return remote(b, b, ss.at[d, s - 1], rs.at[d, s - 1], z_dev[d])

        return send, take

    w1_z, w1_z_in = ring(halves, lambda o: blk(y, o), z_ss, z_rs)

    def slot(i):
        return zat((0, -1, -2, -3, 1, 2, 3, 4)[i])

    def w1_y(d, i):
        b = blk(y, slot(i))
        return remote(b, b, y_ss.at[d, i], y_rs.at[d, i], y_dev[d])

    def w1_y_in(d, i):
        b = blk(yn if d == 0 else yp, slot(i))
        return remote(b, b, y_ss.at[d, i], y_rs.at[d, i], y_dev[d])

    def far_piece(yy, d, j):
        i = (0, 1 + 3 * d, 2 + 3 * d, 3 + 3 * d, 7)[j]
        b = blk(yy, slot(i))
        return halves(b, d) if j in (0, 4) else b

    def w1_f(d, j):
        b = far_piece(yn if d == 0 else yp, d, j)
        return remote(b, b, f_ss.at[d, j], f_rs.at[d, j], y_dev[d])

    yf = (y + 2) % NY

    def w1_f_in(d, j):
        b = far_piece(yf, d, j)
        return remote(b, b, f_ss.at[d, j], f_rs.at[d, j], y_dev[d])

    def share(b, i):
        return remote(b, b, c_ss.at[i], c_rs.at[i], sibling)

    def plane(yy, core):
        return w1.at[pl.ds(yy * 16 + core * 8, 8)]

    def quarter(zz, q):
        return wo.at[zz, 6 + q // 2, pl.ds((q % 2) * 256, 256)]

    def scatter(q):
        return remote(
            quarter(NZ, q), quarter(z, q), q_ss.at[q - 1], q_rs.at[0], device((y + q) % NY, h, z, l, c)
        )

    own_q = pltpu.make_async_copy(quarter(NZ, 0), quarter(z, 0), l_sem.at[5])

    def scatter_in():
        b = quarter(z, rel)
        return remote(b, b, q_ss.at[0], q_rs.at[0], sibling)

    g_z, g_z_in = ring(
        lambda b, d: b.at[pl.ds(128 * d, 128)], lambda o: quarter(o, rel), gz_ss, gz_rs
    )

    def line(yy, k):
        q = (yy + NY - own_t) % NY
        return wo.at[pl.ds(4 * k, 4), 6 + q // 2, pl.ds((q % 2) * 256, 256)]

    def g_y(d, k):
        b = line(y, k)
        return remote(b, b, gy_ss.at[d, k], gy_rs.at[d, k], y_dev[d])

    def g_y_in(d, k):
        b = line(yn if d == 0 else yp, k)
        return remote(b, b, gy_ss.at[d, k], gy_rs.at[d, k], y_dev[d])

    def g_f(d):
        b = line(yn if d == 0 else yp, d)
        return remote(b, b, gy_ss.at[d, 2], gy_rs.at[d, 2], y_dev[d])

    def g_f_in(d):
        b = line(yf, d)
        return remote(b, b, gy_ss.at[d, 2], gy_rs.at[d, 2], y_dev[d])

    def oy(d, k):
        b = wo.at[z, pl.ds(3 * h if k == 0 else 3 - 3 * h, 3)]
        return remote(b, b, oy_ss.at[d, k], oy_rs.at[k], y_dev[d])

    def oz_piece(origin, d, kind):
        if kind == 2:
            return wo.at[origin, pl.ds(3 - 3 * h, 3)]
        return wo.at[origin, pl.ds(3 * h, 3), pl.ds(256 * (d if kind == 0 else 1 - d), 256)]

    def oz(s, d, kind):
        b = oz_piece(zat(1 - s) if d == 0 else zat(s - 1), d, kind)
        return remote(b, b, oz_ss.at[d, s - 1, kind], oz_rs.at[d, s - 1, kind], z_dev[d])

    def oz_in(s, d, kind):
        b = oz_piece(zat(-s) if d == 0 else zat(s), d, kind)
        return remote(b, b, oz_ss.at[d, s - 1, kind], oz_rs.at[d, s - 1, kind], z_dev[d])

    def oz_go(s, kind):
        for d in (0, 1):
            if s > 1:
                oz_in(s - 1, d, kind).wait_recv()
            oz(s, d, kind).start()

    def g_go(s):
        for d in (0, 1):
            if s > 1:
                g_z_in(s - 1, d).wait_recv()
            g_z(s, d).start()

    half_out = wo.at[zat(4), pl.ds(3 * h, 3)]
    half_in = wo.at[zat(4), pl.ds(3 * (1 - h), 3)]
    far_out = remote(half_out, half_out, x2_ss.at[0], x2_rs.at[0], device(y, 1 - h, z, l, c))
    far_in = remote(half_in, half_in, x2_ss.at[0], x2_rs.at[0], device(y, 1 - h, z, l, c))

    @pl.when(main)
    def _():
        own1.wait()

    @pl.when(jnp.logical_not(main))
    def _():
        exchange_in.wait_recv()

    for d in (0, 1):
        w1_z(1, d).start()

    @pl.when(source)
    def _():
        own_o.wait()
        for u in range(8):
            @pl.when(u != 2 * own_t + h)
            def _():
                remote(wo_own, wo.at[z if u < 6 else NZ, u], ox_ss.at[0], ox_rs.at[u], sibling).wait_recv()
        own_q.start()
        for q in (1, 3, 2):
            scatter(q).start()
        for k in (0, 1):
            for d in (0, 1):
                oy(d, k).start()

    later = (jnp.logical_and(rel == 1, c == 1), jnp.logical_and(rel == 3, c == 0))

    def y_start(group, *ways):
        for d in (0, 1):
            @pl.when(ways[d])
            def _():
                for i in group:
                    w1_y(d, i).start()

    at_once = tuple(jnp.logical_not(v) for v in later)
    y_start((0,), *at_once)
    for s in (2, 3, 4):
        for d in (0, 1):
            w1_z_in(s - 1, d).wait_recv()
            w1_z(s, d).start()
        if s < 4:
            k = s - 2

            @pl.when(jnp.logical_or(rel == 1, rel == 3))
            def _():
                oy(0, k).wait_recv()

            for d in (0, 1):
                @pl.when(later[d])
                def _():
                    oy(d, k).start()

        if s == 2:
            y_start((1, 4), *at_once)
        if s == 3:
            y_start((0, 1, 4), *later)

            @pl.when(jnp.logical_not(source))
            def _():
                scatter_in().wait_recv()

            @pl.when(source)
            def _():
                own_q.wait()

            g_go(1)

    g_go(2)
    for i in (2, 5, 3, 6):
        for d in (0, 1):
            w1_y(d, i).start()

    for d in (0, 1):
        w1_z_in(4, d).wait_recv()
    for d in (0, 1):
        w1_y(d, 7).start()
    share(plane(y, c), 0).start()
    g_go(3)

    @pl.when(rel == 2)
    def _():
        oy(0, 0).wait_recv()

    oz_go(1, 0)
    oz_go(1, 1)

    @pl.when(rel == 2)
    def _():
        oy(0, 1).wait_recv()

    oz_go(1, 2)

    def y_group(group, j):
        for d in (0, 1):
            for i in group:
                w1_y_in(d, i).wait_recv()
            w1_f(d, j).start()

    for j in (0, 1):
        got_tok(2 * near_pair + j, fwd_half).wait_recv()
        tok_forward(j).start()
    g_go(4)
    oz_go(2, 0)
    y_group((0,), 0)
    y_group((1, 4), 1)
    oz_go(3, 0)
    oz_go(2, 2)
    y_group((2, 5), 2)
    oz_go(4, 0)
    oz_go(2, 1)
    y_group((3, 6), 3)
    y_group((7,), 4)
    share(plane(yn, c), 1).start()
    share(plane(yp, c), 2).start()
    for d in (0, 1):
        g_z_in(4, d).wait_recv()
    for d in (0, 1):
        for k in (0, 1):
            g_y(d, k if d == 0 else 1 - k).start()
    gain[...] = gain_in[...].astype(jnp.float32).reshape(1, 4 * FEATS)
    acc[...] = jnp.zeros_like(acc)
    ssq[...] = jnp.zeros_like(ssq)

    def project(f):
        def body(i, _):
            cols = pl.ds(pl.multiple_of(i * 512, 512), 512)
            xf = xb[f, :, cols].astype(jnp.float32)
            sq = xf * xf
            ssq[...] += sq[:, :128] + sq[:, 128:256] + sq[:, 256:384] + sq[:, 384:]
            g = gain[:, pl.ds(pl.multiple_of(f * FEATS + i * 512, 512), 512)]
            xg = (xf * g).astype(jnp.bfloat16)
            w = w1[pl.ds(f * 16 + i * 4, 4)].reshape(512, 768)
            acc[...] += jnp.dot(xg, w, preferred_element_type=jnp.float32)
            return 0

        lax.fori_loop(0, 4, body, 0)

    keep_tok.start()

    def tokens_here(f):
        own = jnp.logical_and(main, f == own_t)

        @pl.when(own)
        def _():
            own_tok.wait()

        for k in (0, 1):
            handed = jnp.logical_and(f // 2 == near_pair, k == fwd_half)

            @pl.when(jnp.logical_not(jnp.logical_or(own, handed)))
            def _():
                got_tok(f, k).wait_recv()

    share(plane(y, 1 - c), 0).wait_recv()
    tokens_here(y)
    project(y)
    oz_go(3, 2)
    share(plane(yn, 1 - c), 1).wait_recv()
    tokens_here(yn)
    project(yn)
    oz_go(3, 1)
    share(plane(yp, 1 - c), 2).wait_recv()
    tokens_here(yp)
    project(yp)
    for d in (0, 1):
        oz_in(4, d, 0).wait_recv()
    far_out.start()

    def far_share(yy, core, d, j):
        i = (0, 1 + 3 * d, 2 + 3 * d, 3 + 3 * d, 7)[j]
        b = w1.at[yy * 16 + core * 8 + slot(i)]
        return share(halves(b, d) if j in (0, 4) else b, 3 + 5 * d + j)

    for j in range(5):
        for d in (0, 1):
            w1_f_in(d, j).wait_recv()
            far_share(yf, c, d, j).start()
    for j in range(5):
        for d in (0, 1):
            far_share(yf, 1 - c, d, j).wait_recv()
    tokens_here(yf)
    project(yf)

    @pl.when(main)
    def _():
        own_len.wait()

    @pl.when(jnp.logical_not(main))
    def _():
        remote(len_own, lenb, n_ss.at[0], n_rs.at[0], partner).wait_recv()

    rs = lax.rsqrt(jnp.sum(ssq[...], axis=1, keepdims=True) * (1.0 / 8192.0) + 1e-05)

    def rotate(v):
        return (v * cos[...] + pltpu.roll(v, 64, 1) * sin[...]).astype(jnp.bfloat16)

    rk = rotate(acc[:, 512:640] * rs)
    rv = (acc[:, 640:768] * rs).astype(jnp.bfloat16)
    i_pos = lax.broadcasted_iota(jnp.int32, (SEQ, SEQ), 0)
    j_pos = lax.broadcasted_iota(jnp.int32, (SEQ, SEQ), 1)
    keep = jnp.logical_and(j_pos <= i_pos, j_pos < lenb[0:1, 0:1])
    scale = 1.0 / float(np.sqrt(128.0))
    t_here = 2 * l + h

    def a_self(ld):
        return jnp.logical_and(main, l == ld)

    def a_out(ld, hd):
        return remote(aout.at[hd], ab.at[t_here, hd], a_ss.at[ld, hd], a_rs.at[t_here, hd], device(y, c, z, ld, c))

    def a_in(t, hd):
        return remote(aout.at[hd], ab.at[t, hd], a_ss.at[0, hd], a_rs.at[t, hd], sibling)

    def b_copy(t, hd):
        return remote(ab.at[t, hd], ab.at[t, hd], b_ss.at[t, hd], b_rs.at[t, hd], sibling)

    for hd in range(HEADS):
        rq = rotate(acc[:, hd * HEAD : (hd + 1) * HEAD] * rs)
        s = lax.dot_general(rq, rk, (((1,), (1,)), ((), ())), preferred_element_type=jnp.float32) * scale
        s = jnp.where(keep, s, jnp.float32(-1e30))
        e = jnp.exp(s - jnp.max(s, axis=1, keepdims=True))
        total = jnp.sum(e, axis=1, keepdims=True)
        o = jnp.dot(e.astype(jnp.bfloat16), rv, preferred_element_type=jnp.float32) / total
        o = o.astype(jnp.bfloat16)
        aout[hd] = o
        for ld in (0, 1):
            @pl.when(jnp.logical_not(a_self(ld)))
            def _():
                a_out(ld, hd).start()

        @pl.when(main)
        def _():
            ab[t_here, hd] = o
            b_copy(t_here, hd).start()

        if hd == 1:
            for d in (0, 1):
                g_y_in(d, d).wait_recv()
                g_f(d).start()

    def attended_here(t):
        for hd in range(HEADS):
            @pl.when(jnp.logical_and(main, t != t_here))
            def _():
                a_in(t, hd).wait_recv()
                b_copy(t, hd).start()

            @pl.when(jnp.logical_not(main))
            def _():
                b_copy(t, hd).wait_recv()

    def product(zz, t):
        a = jnp.concatenate([ab[t, hd] for hd in range(HEADS)], axis=1)
        w = jnp.concatenate([wo[zz, 2 * t], wo[zz, 2 * t + 1]], axis=1)
        return jnp.dot(a, w, preferred_element_type=jnp.float32)

    def start_out(zz, _):
        for hh in (0, 1):
            cols = pl.ds(pl.multiple_of(hh * 1024 + zz * 128, 128), 128)
            mixed[zz, :, hh * 128 : (hh + 1) * 128] = tok_own[:, cols].astype(jnp.float32)
        return 0

    keep_tok.wait()
    lax.fori_loop(0, NZ, start_out, 0)
    for i in range(3):
        t = (t_here + i) % 3
        attended_here(t)

        def near_body(j, _, t=t):
            zz = (z + j + NZ - 2) % NZ
            mixed[zz] += product(zz, t)
            return 0

        lax.fori_loop(0, 5, near_body, 0)
    attended_here(3)
    for d in (0, 1):
        for kind in (1, 2):
            oz_in(3, d, kind).wait_recv()
    far_in.wait_recv()

    def rest_body(j, _):
        zz = (z + j + 3) % NZ
        mixed[zz] += product(zz, 0) + product(zz, 1) + product(zz, 2)
        return 0

    lax.fori_loop(0, 3, rest_body, 0)
    for d in (0, 1):
        g_y_in(d, 1 - d).wait_recv()
        g_f_in(d).wait_recv()

    def last_body(zz, _):
        total = mixed[zz] + product(zz, 3)
        for hh in (0, 1):
            cols = pl.ds(pl.multiple_of(hh * 1024 + zz * 128, 128), 128)
            out[:, cols] = total[:, hh * 128 : (hh + 1) * 128].astype(jnp.bfloat16)
        return 0

    lax.fori_loop(0, NZ, last_body, 0)

    @pl.when(jnp.logical_not(main))
    def _():
        exchange.wait_send()
        len_out.wait_send()
        tok_copy(x, 0, 2).wait_send()
        tok_copy(x, 1, 2).wait_send()

    for hd in (0, 1):
        @pl.when(jnp.logical_not(jnp.logical_and(source, h == hd)))
        def _():
            ox[hd].wait_send()
    for k in (0, 1):
        tok_copy(pair_x, k, 0).wait_send()
        tok_copy(outer_x, k, 1).wait_send()
        tok_forward(k).wait_send()
    for d in (0, 1):
        for i in range(8):
            w1_y(d, i).wait_send()
        for j in range(5):
            w1_f(d, j).wait_send()
            far_share(yf, c, d, j).wait_send()
        for s in (1, 2, 3, 4):
            w1_z(s, d).wait_send()
            g_z(s, d).wait_send()
        for k in (0, 1):
            g_y(d, k).wait_send()
        for s in (1, 2, 3):
            for kind in (0, 1, 2):
                oz(s, d, kind).wait_send()
        oz(4, d, 0).wait_send()
        g_f(d).wait_send()
    far_out.wait_send()
    share(plane(y, c), 0).wait_send()
    share(plane(yn, c), 1).wait_send()
    share(plane(yp, c), 2).wait_send()

    @pl.when(source)
    def _():
        for q in (1, 2, 3):
            scatter(q).wait_send()
        for d in (0, 1):
            for k in (0, 1):
                oy(d, k).wait_send()

    for k in (0, 1):
        @pl.when(jnp.logical_and(rel == 1, c == 1))
        def _():
            oy(0, k).wait_send()

        @pl.when(jnp.logical_and(rel == 3, c == 0))
        def _():
            oy(1, k).wait_send()

    for hd in range(HEADS):
        for ld in (0, 1):
            @pl.when(jnp.logical_not(a_self(ld)))
            def _():
                a_out(ld, hd).wait_send()

        @pl.when(main)
        def _():
            for t in range(4):
                b_copy(t, hd).wait_send()


def per_device(tokens, norm_gain, q_weight, key_value_weight, output_weight, lengths):
    cosine, sine = rotary_tables()
    dma = pltpu.SemaphoreType.DMA
    vmem = pl.BlockSpec(memory_space=pltpu.VMEM)
    bf16 = jnp.bfloat16
    return pl.pallas_call(
        kernel,
        out_shape=jax.ShapeDtypeStruct((SEQ, FEATS), bf16),
        in_specs=[pl.BlockSpec(memory_space=pl.ANY)] + [vmem] * 4 + [pl.BlockSpec(memory_space=pltpu.SMEM)] + [vmem] * 2,
        out_specs=vmem,
        scratch_shapes=[
            pltpu.VMEM((SEQ, FEATS), bf16),
            pltpu.VMEM((1, 4 * FEATS), jnp.float32),
            pltpu.VMEM((128, 768), bf16),
            pltpu.VMEM((8, 128), jnp.int32),
            pltpu.VMEM((4, SEQ, FEATS), bf16),
            pltpu.VMEM((64, 128, 768), bf16),
            pltpu.VMEM((NZ + 1, 8, 512, 128), bf16),
            pltpu.VMEM((4, HEADS, SEQ, HEAD), bf16),
            pltpu.VMEM((HEADS, SEQ, HEAD), bf16),
            pltpu.VMEM((8, 128), jnp.int32),
            pltpu.VMEM((SEQ, 768), jnp.float32),
            pltpu.VMEM((SEQ, 128), jnp.float32),
            pltpu.VMEM((NZ, SEQ, 256), jnp.float32),
            dma((3, 2)), dma((4, 2)), dma((2,)), dma((6,)), dma((1,)), dma((1,)), dma((1,)), dma((1,)),
            dma((2, 4)), dma((2, 4)), dma((2, 8)), dma((2, 8)), dma((2, 5)), dma((2, 5)), dma((13,)), dma((13,)),
            dma((2,)), dma((8,)), dma((2, 2)), dma((2,)), dma((2, 4, 3)), dma((2, 4, 3)),
            dma((3,)), dma((1,)), dma((2, 4)), dma((2, 4)), dma((2, 3)), dma((2, 3)), dma((1,)), dma((1,)),
            dma((2, HEADS)), dma((4, HEADS)), dma((4, HEADS)), dma((4, HEADS)),
        ],
        compiler_params=pltpu.CompilerParams(
            collective_id=0, has_side_effects=True, vmem_limit_bytes=56 * 2**20
        ),
        cost_estimate=pl.CostEstimate(flops=8 * 10**9, bytes_accessed=4 * 2**20, transcendentals=600000),
    )(tokens, norm_gain, q_weight, key_value_weight, output_weight, lengths, jnp.asarray(cosine), jnp.asarray(sine))


def solution(mesh):
    return jax.shard_map(
        per_device,
        mesh=mesh,
        in_specs=(
            P("dp", "tensor"),
            P(),
            P("dp", "tensor"),
            P("dp", None, "tensor"),
            P("tensor", "dp"),
            P("dp"),
        ),
        out_specs=P("dp", "tensor"),
        check_vma=False,
    )
```

time: 131 us -> 125 us (0.954)
  other arithmetic: 2.91 us -> 0 us
  local copies, waits for them, and re-layouts: 4.17 us -> 2.73 us
    concatenate x1 -> x0, other arithmetic: 1.6 us -> none  [per_device(): jnp.concatenate([q_weight, key_value_weight.reshape(128, 256)], axis=1)]
    reshape x1 -> x0, other arithmetic: 1.32 us -> none  [per_device(): gain = norm_gain.astype(jnp.float32).reshape(4, 1, FEATS)]
    unnamed x2 -> x1, local copies, waits for them, and re-layouts: 3.58 us -> 2.73 us
where the time goes in v2:
time: 125 us
  Pallas kernels  121 us (97%)
  local copies, waits for them, and re-layouts  2.73 us (2%)
    pallas_call x1, Pallas kernels, per_device(): pl.pallas_call(kernel, out_shape=jax.ShapeDtypeStruct((SEQ, FEATS), bf16)...  121 us
    unnamed x1, local copies, waits for them, and re-layouts  2.73 us

profile of v2, /device:TPU:1, one launch (start us, length us, event | category | flops | bytes accessed | tf_op | source)
XLA Modules:
  0.0 124.5 jit_solution(8919865175570859991)
XLA Ops:
  0.7 121.1 %shard_map.82 = bf16[384,2048]{1,0:T(8,128)(2,1)} custom-call(bf16[384,2048]{1,0:T(8,128)(2,1)} %tok.1, bf16[8192]{0:T(1024)(128)(2,1)} %gain_in.1, bf16[128,512]{1,0:T(8,128)(2,1)} %q_own.1, bf16[128,2,128]{2,1,0:T(2,128)(2,1)} %kv_own.1, bf16[512,128]{1,0:T(8,128)(2,1)} %wo_own.1, s32[1]{0:T(128)S(6)} %copy.10.length, f32[384,128]{1,0:T(8,128)} %constant.4.clone.cos, ...), custom_call_target="tpu_custom_call" | custom-call | flops 8000000000 | bytes 4194304 | tf_op jit(solution)/shard_map/pallas_call | solution.py:651
  121.8 2.7 %copy.11 = bf16[384,2048]{1,0:T(8,128)(2,1)} copy(bf16[384,2048]{1,0:T(8,128)(2,1)} %shard_map.82) | data formatting | bytes 3145728

commit v3 on v2

--- a/solution.py
+++ b/solution.py
@@ -33,7 +33,7 @@
 
 def kernel(
     tok, gain_in, q_own, kv_own, wo_own, length, cos, sin, out,
-    tok_own, gain, w1_own, len_own, xb, w1, wo, ab, aout, lenb, acc, ssq, mixed,
+    tok_own, gain, w1_own, len_own, xb, w1, wo, ab, aout, lenb, acc, ssq, scaled, mixed,
     t_ss, t_rs, t_fs, l_sem, e_ss, e_rs, n_ss, n_rs,
     z_ss, z_rs, y_ss, y_rs, f_ss, f_rs, c_ss, c_rs,
     ox_ss, ox_rs, oy_ss, oy_rs, oz_ss, oz_rs,
@@ -71,12 +71,12 @@
             partners.append(at_x((x + k) % 4, cc))
     for p in partners:
         pl.semaphore_signal(barrier, inc=1, device_id=p, device_id_type=MESH)
-    pl.semaphore_wait(barrier, len(partners))
-
     w1_own[:, :512] = q_own[...]
     w1_own[:, 512:640] = kv_own[:, 0, :]
     w1_own[:, 640:] = kv_own[:, 1, :]
     len_own[...] = jnp.full((8, 128), length[0], jnp.int32)
+    pl.semaphore_wait(barrier, len(partners))
+
     me1 = y * 16 + c * 8 + z
     partner = device(y, 1 - h, z, l, 1 - c)
     exchange = remote(w1_own, w1.at[y * 16 + (1 - c) * 8 + z], e_ss.at[0], e_rs.at[0], partner)
@@ -365,11 +365,6 @@
     oz_go(1, 0)
     oz_go(1, 1)
 
-    @pl.when(rel == 2)
-    def _():
-        oy(0, 1).wait_recv()
-
-    oz_go(1, 2)
 
     def y_group(group, j):
         for d in (0, 1):
@@ -381,15 +376,21 @@
         got_tok(2 * near_pair + j, fwd_half).wait_recv()
         tok_forward(j).start()
     g_go(4)
+    y_group((0,), 0)
     oz_go(2, 0)
-    y_group((0,), 0)
+
+    @pl.when(rel == 2)
+    def _():
+        oy(0, 1).wait_recv()
+
+    oz_go(1, 2)
     y_group((1, 4), 1)
     oz_go(3, 0)
+    oz_go(2, 1)
+    y_group((2, 5), 2)
+    y_group((3, 6), 3)
+    oz_go(4, 0)
     oz_go(2, 2)
-    y_group((2, 5), 2)
-    oz_go(4, 0)
-    oz_go(2, 1)
-    y_group((3, 6), 3)
     y_group((7,), 4)
     share(plane(yn, c), 1).start()
     share(plane(yp, c), 2).start()
@@ -416,6 +417,27 @@
 
         lax.fori_loop(0, 4, body, 0)
 
+    def prepare(f):
+        def body(i, _):
+            cols = pl.ds(pl.multiple_of(i * 512, 512), 512)
+            xf = xb[f, :, cols].astype(jnp.float32)
+            sq = xf * xf
+            ssq[...] += sq[:, :128] + sq[:, 128:256] + sq[:, 256:384] + sq[:, 384:]
+            g = gain[:, pl.ds(pl.multiple_of(f * FEATS + i * 512, 512), 512)]
+            scaled[:, cols] = (xf * g).astype(jnp.bfloat16)
+            return 0
+
+        lax.fori_loop(0, 4, body, 0)
+
+    def project_prepared(f):
+        def body(i, _):
+            cols = pl.ds(pl.multiple_of(i * 512, 512), 512)
+            w = w1[pl.ds(f * 16 + i * 4, 4)].reshape(512, 768)
+            acc[...] += jnp.dot(scaled[:, cols], w, preferred_element_type=jnp.float32)
+            return 0
+
+        lax.fori_loop(0, 4, body, 0)
+
     keep_tok.start()
 
     def tokens_here(f):
@@ -435,17 +457,27 @@
     share(plane(y, 1 - c), 0).wait_recv()
     tokens_here(y)
     project(y)
-    oz_go(3, 2)
+    oz_go(3, 1)
     share(plane(yn, 1 - c), 1).wait_recv()
     tokens_here(yn)
     project(yn)
-    oz_go(3, 1)
+    for d in (0, 1):
+        oz_in(4, d, 0).wait_recv()
+    far_out.start()
     share(plane(yp, 1 - c), 2).wait_recv()
     tokens_here(yp)
     project(yp)
-    for d in (0, 1):
-        oz_in(4, d, 0).wait_recv()
-    far_out.start()
+    tokens_here(yf)
+    prepare(yf)
+
+    def start_out(zz, _):
+        for hh in (0, 1):
+            cols = pl.ds(pl.multiple_of(hh * 1024 + zz * 128, 128), 128)
+            mixed[zz, :, hh * 128 : (hh + 1) * 128] = tok_own[:, cols].astype(jnp.float32)
+        return 0
+
+    keep_tok.wait()
+    lax.fori_loop(0, NZ, start_out, 0)
 
     def far_share(yy, core, d, j):
         i = (0, 1 + 3 * d, 2 + 3 * d, 3 + 3 * d, 7)[j]
@@ -459,8 +491,8 @@
     for j in range(5):
         for d in (0, 1):
             far_share(yf, 1 - c, d, j).wait_recv()
-    tokens_here(yf)
-    project(yf)
+    oz_go(3, 2)
+    project_prepared(yf)
 
     @pl.when(main)
     def _():
@@ -514,63 +546,53 @@
             ab[t_here, hd] = o
             b_copy(t_here, hd).start()
 
-        if hd == 1:
+    for d in (0, 1):
+        g_y_in(d, d).wait_recv()
+        g_f(d).start()
+
+    def attended_here(t, hd):
+        @pl.when(jnp.logical_and(main, t != t_here))
+        def _():
+            a_in(t, hd).wait_recv()
+            b_copy(t, hd).start()
+
+        @pl.when(jnp.logical_not(main))
+        def _():
+            b_copy(t, hd).wait_recv()
+
+    def product(zz, groups, heads):
+        n = len(heads) * HEAD
+        rows_w = pl.ds(heads[0] * HEAD, n)
+        a = jnp.concatenate([ab[t, hd] for t in groups for hd in heads], axis=1)
+        w = jnp.concatenate(
+            [jnp.concatenate([wo[zz, 2 * t, rows_w], wo[zz, 2 * t + 1, rows_w]], axis=1) for t in groups], axis=0
+        )
+        return jnp.dot(a, w, preferred_element_type=jnp.float32)
+
+    for part in (0, 1):
+        heads = (2 * part, 2 * part + 1)
+        for hd in heads:
+            for t in range(4):
+                attended_here(t, hd)
+
+        def out_body(j, _, heads=heads):
+            zz = (z + j + NZ - 2) % NZ
+            mixed[zz] += product(zz, (0, 1, 2), heads)
+            return 0
+
+        lax.fori_loop(0, 5, out_body, 0)
+        if part == 0:
             for d in (0, 1):
-                g_y_in(d, d).wait_recv()
-                g_f(d).start()
-
-    def attended_here(t):
-        for hd in range(HEADS):
-            @pl.when(jnp.logical_and(main, t != t_here))
-            def _():
-                a_in(t, hd).wait_recv()
-                b_copy(t, hd).start()
-
-            @pl.when(jnp.logical_not(main))
-            def _():
-                b_copy(t, hd).wait_recv()
-
-    def product(zz, t):
-        a = jnp.concatenate([ab[t, hd] for hd in range(HEADS)], axis=1)
-        w = jnp.concatenate([wo[zz, 2 * t], wo[zz, 2 * t + 1]], axis=1)
-        return jnp.dot(a, w, preferred_element_type=jnp.float32)
-
-    def start_out(zz, _):
-        for hh in (0, 1):
-            cols = pl.ds(pl.multiple_of(hh * 1024 + zz * 128, 128), 128)
-            mixed[zz, :, hh * 128 : (hh + 1) * 128] = tok_own[:, cols].astype(jnp.float32)
-        return 0
-
-    keep_tok.wait()
-    lax.fori_loop(0, NZ, start_out, 0)
-    for i in range(3):
-        t = (t_here + i) % 3
-        attended_here(t)
-
-        def near_body(j, _, t=t):
-            zz = (z + j + NZ - 2) % NZ
-            mixed[zz] += product(zz, t)
-            return 0
-
-        lax.fori_loop(0, 5, near_body, 0)
-    attended_here(3)
-    for d in (0, 1):
-        for kind in (1, 2):
-            oz_in(3, d, kind).wait_recv()
-    far_in.wait_recv()
-
-    def rest_body(j, _):
-        zz = (z + j + 3) % NZ
-        mixed[zz] += product(zz, 0) + product(zz, 1) + product(zz, 2)
-        return 0
-
-    lax.fori_loop(0, 3, rest_body, 0)
+                for kind in (1, 2):
+                    oz_in(3, d, kind).wait_recv()
+            far_in.wait_recv()
+        lax.fori_loop(5, NZ, out_body, 0)
     for d in (0, 1):
         g_y_in(d, 1 - d).wait_recv()
         g_f_in(d).wait_recv()
 
     def last_body(zz, _):
-        total = mixed[zz] + product(zz, 3)
+        total = mixed[zz] + product(zz, (3,), (0, 1, 2, 3))
         for hh in (0, 1):
             cols = pl.ds(pl.multiple_of(hh * 1024 + zz * 128, 128), 128)
             out[:, cols] = total[:, hh * 128 : (hh + 1) * 128].astype(jnp.bfloat16)
@@ -666,6 +688,7 @@
             pltpu.VMEM((8, 128), jnp.int32),
             pltpu.VMEM((SEQ, 768), jnp.float32),
             pltpu.VMEM((SEQ, 128), jnp.float32),
+            pltpu.VMEM((SEQ, FEATS), bf16),
             pltpu.VMEM((NZ, SEQ, 256), jnp.float32),
             dma((3, 2)), dma((4, 2)), dma((2,)), dma((6,)), dma((1,)), dma((1,)), dma((1,)), dma((1,)),
             dma((2, 4)), dma((2, 4)), dma((2, 8)), dma((2, 8)), dma((2, 5)), dma((2, 5)), dma((13,)), dma((13,)),

time: 125 us -> 116 us (0.928)
  Pallas kernels: 121 us -> 111 us
    pallas_call x1, Pallas kernels: 121 us -> 111 us  [per_device(): pl.pallas_call(kernel, out_shape=jax.ShapeDtypeStruct((SEQ, FEATS), bf16)...]
where the time goes in v3:
time: 116 us; the launch traced here: 115 us
  Pallas kernels  111 us (96%)
  local copies, waits for them, and re-layouts  2.73 us (2%)
    pallas_call x1, Pallas kernels, per_device(): pl.pallas_call(kernel, out_shape=jax.ShapeDtypeStruct((SEQ, FEATS), bf16)...  111 us
    unnamed x1, local copies, waits for them, and re-layouts  2.73 us

profile of v3, /device:TPU:1, one launch (start us, length us, event | category | flops | bytes accessed | tf_op | source)
XLA Modules:
  0.0 114.7 jit_solution(14207351277599803274)
XLA Ops:
  0.7 111.3 %shard_map.82 = bf16[384,2048]{1,0:T(8,128)(2,1)} custom-call(bf16[384,2048]{1,0:T(8,128)(2,1)} %tok.1, bf16[8192]{0:T(1024)(128)(2,1)} %gain_in.1, bf16[128,512]{1,0:T(8,128)(2,1)} %q_own.1, bf16[128,2,128]{2,1,0:T(2,128)(2,1)} %kv_own.1, bf16[512,128]{1,0:T(8,128)(2,1)} %wo_own.1, s32[1]{0:T(128)S(6)} %copy.10.length, f32[384,128]{1,0:T(8,128)} %constant.4.clone.cos, ...), custom_call_target="tpu_custom_call" | custom-call | flops 8000000000 | bytes 4194304 | tf_op jit(solution)/shard_map/pallas_call | solution.py:673
  112.0 2.7 %copy.11 = bf16[384,2048]{1,0:T(8,128)(2,1)} copy(bf16[384,2048]{1,0:T(8,128)(2,1)} %shard_map.82) | data formatting | bytes 3145728

commit v4 on v3

--- a/solution.py
+++ b/solution.py
@@ -672,7 +672,7 @@
     bf16 = jnp.bfloat16
     return pl.pallas_call(
         kernel,
-        out_shape=jax.ShapeDtypeStruct((SEQ, FEATS), bf16),
+        out_shape=pltpu.VMEM((SEQ, FEATS), bf16),
         in_specs=[pl.BlockSpec(memory_space=pl.ANY)] + [vmem] * 4 + [pl.BlockSpec(memory_space=pltpu.SMEM)] + [vmem] * 2,
         out_specs=vmem,
         scratch_shapes=[

time: 116 us -> 113 us (0.974)
  local copies, waits for them, and re-layouts: 2.73 us -> 1.15 us
    unnamed x1, local copies, waits for them, and re-layouts: 2.73 us -> 1.15 us
where the time goes in v4:
time: 113 us; the launch traced here: 112 us
  Pallas kernels  110 us (97%)
  local copies, waits for them, and re-layouts  1.15 us (1%)
    pallas_call x1, Pallas kernels, per_device(): pl.pallas_call(kernel, out_shape=pltpu.VMEM((SEQ, FEATS), bf16), in_specs...  110 us

profile of v4, /device:TPU:1, one launch (start us, length us, event | category | flops | bytes accessed | tf_op | source)
XLA Modules:
  0.0 112.0 jit_solution(18060447204521439159)
XLA Ops:
  0.7 110.2 %shard_map.82 = bf16[384,2048]{1,0:T(8,128)(2,1)S(1)} custom-call(bf16[384,2048]{1,0:T(8,128)(2,1)} %tok.1, bf16[8192]{0:T(1024)(128)(2,1)} %gain_in.1, bf16[128,512]{1,0:T(8,128)(2,1)} %q_own.1, bf16[128,2,128]{2,1,0:T(2,128)(2,1)} %kv_own.1, bf16[512,128]{1,0:T(8,128)(2,1)} %wo_own.1, s32[1]{0:T(128)S(6)} %copy.11.length, f32[384,128]{1,0:T(8,128)} %constant.4.clone.cos, ...), custom_call_target="tpu_custom_call" | custom-call | flops 8000000000 | bytes 4194304 | tf_op jit(solution)/shard_map/pallas_call | solution.py:673
  110.8 1.1 %copy.10 = bf16[384,2048]{1,0:T(8,128)(2,1)} copy(bf16[384,2048]{1,0:T(8,128)(2,1)S(1)} %shard_map.82) | data formatting | bytes 3145728

commit v5 on v4

--- a/solution.py
+++ b/solution.py
@@ -372,12 +372,12 @@
                 w1_y_in(d, i).wait_recv()
             w1_f(d, j).start()
 
+    g_go(4)
+    oz_go(2, 0)
+    y_group((0,), 0)
     for j in (0, 1):
         got_tok(2 * near_pair + j, fwd_half).wait_recv()
         tok_forward(j).start()
-    g_go(4)
-    y_group((0,), 0)
-    oz_go(2, 0)
 
     @pl.when(rel == 2)
     def _():
@@ -580,19 +580,19 @@
             mixed[zz] += product(zz, (0, 1, 2), heads)
             return 0
 
-        lax.fori_loop(0, 5, out_body, 0)
         if part == 0:
+            lax.fori_loop(0, 5, out_body, 0)
             for d in (0, 1):
                 for kind in (1, 2):
                     oz_in(3, d, kind).wait_recv()
             far_in.wait_recv()
-        lax.fori_loop(5, NZ, out_body, 0)
+            lax.fori_loop(5, NZ, out_body, 0)
     for d in (0, 1):
         g_y_in(d, 1 - d).wait_recv()
         g_f_in(d).wait_recv()
 
     def last_body(zz, _):
-        total = mixed[zz] + product(zz, (3,), (0, 1, 2, 3))
+        total = mixed[zz] + product(zz, (0, 1, 2), (2, 3)) + product(zz, (3,), (0, 1, 2, 3))
         for hh in (0, 1):
             cols = pl.ds(pl.multiple_of(hh * 1024 + zz * 128, 128), 128)
             out[:, cols] = total[:, hh * 128 : (hh + 1) * 128].astype(jnp.bfloat16)

time: 113 us -> 112 us (level)
    pallas_call x1, Pallas kernels: 110 us -> 109 us  [per_device(): pl.pallas_call(kernel, out_shape=pltpu.VMEM((SEQ, FEATS), bf16), in_specs...]
where the time goes in v5:
time: 112 us; the launch traced here: 111 us
  Pallas kernels  109 us (97%)
  local copies, waits for them, and re-layouts  1.15 us (1%)
    pallas_call x1, Pallas kernels, per_device(): pl.pallas_call(kernel, out_shape=pltpu.VMEM((SEQ, FEATS), bf16), in_specs...  109 us

profile of v5, /device:TPU:1, one launch (start us, length us, event | category | flops | bytes accessed | tf_op | source)
XLA Modules:
  0.0 110.7 jit_solution(947861333759422462)
XLA Ops:
  0.7 108.9 %shard_map.82 = bf16[384,2048]{1,0:T(8,128)(2,1)S(1)} custom-call(bf16[384,2048]{1,0:T(8,128)(2,1)} %tok.1, bf16[8192]{0:T(1024)(128)(2,1)} %gain_in.1, bf16[128,512]{1,0:T(8,128)(2,1)} %q_own.1, bf16[128,2,128]{2,1,0:T(2,128)(2,1)} %kv_own.1, bf16[512,128]{1,0:T(8,128)(2,1)} %wo_own.1, s32[1]{0:T(128)S(6)} %copy.11.length, f32[384,128]{1,0:T(8,128)} %constant.4.clone.cos, ...), custom_call_target="tpu_custom_call" | custom-call | flops 8000000000 | bytes 4194304 | tf_op jit(solution)/shard_map/pallas_call | solution.py:673
  109.5 1.1 %copy.10 = bf16[384,2048]{1,0:T(8,128)(2,1)} copy(bf16[384,2048]{1,0:T(8,128)(2,1)S(1)} %shard_map.82) | data formatting | bytes 3145728
